TPU v7x, 512 devices: a whole 4x4x16 slice. The times are simulated.
512 devices in a mesh: band: 64 (over x, z_lo, core), kpt: 8 (over z_hi, y).
Axes of the slice: x: 4, y: 4, z: 16 (z_hi: 2, z_lo: 8; z = z_hi * 8 + z_lo), core: 2. Of those that a mesh axis runs over, the one named last changes fastest.
Arguments:
- orbitals: bfloat16 [8, 128, 2, 48, 2304], P('kpt', 'band'), may hold values from -6 to 6
- kpoint_offsets: int32 [8, 3], replicated, may hold values from 0 to 1
- umklapp: int32 [8, 2, 3], P('kpt'), may hold values from -1 to 1
Outputs:
- exchange_applied: bfloat16 [8, 128, 2, 48, 2304], P('kpt', 'band')
All inputs are finite; a program needn't handle non-finite values.
Results may differ from a plain program's by a relative error of at most 0.023.
Values may be sent and summed in bfloat16 or wider, within the bound.
A program may use at most 128 MiB of HBM per device.

v0:
```python
import math

import jax
import jax.numpy as jnp
from jax import lax
from jax.sharding import PartitionSpec as P

KSTEPS = 2


def from_behind(value, axis, by):
    count = lax.axis_size(axis)
    return lax.ppermute(value, axis, [(i, (i + by) % count) for i in range(count)])


def from_root(value, axis, root):
    mine = lax.axis_index(axis) == root
    return lax.psum(jnp.where(mine, value, jnp.zeros_like(value)), axis)


def section_table(count, inverse):
    idx = jnp.arange(count, dtype=jnp.int32)
    phase = (idx[:, None] * idx[None, :] % count).astype(jnp.float32) * (2.0 * math.pi / count)
    scale = 1.0 / math.sqrt(count)
    cos_tab = (jnp.cos(phase) * scale).astype(jnp.bfloat16)
    sin_tab = (jnp.sin(phase) * scale).astype(jnp.bfloat16)
    if inverse:
        upper = jnp.concatenate([cos_tab, -sin_tab], axis=1)
        lower = jnp.concatenate([sin_tab, cos_tab], axis=1)
    else:
        upper = jnp.concatenate([cos_tab, sin_tab], axis=1)
        lower = jnp.concatenate([-sin_tab, cos_tab], axis=1)
    return jnp.concatenate([upper, lower], axis=0)


def transform(parts, table):
    count = parts.shape[1]
    for section in range(3):
        flat = parts.reshape(2 * count, count * count)
        product = jnp.dot(table, flat, preferred_element_type=jnp.float32).astype(jnp.bfloat16)
        parts = (
            product.reshape(2, count, count, count)
            .transpose(0, 2, 3, 1)
            .reshape(2, count, count * count)
        )
    return parts


def screening(qvec, count):
    freq = ((jnp.arange(count, dtype=jnp.int32) + count // 2) % count - count // 2).astype(
        jnp.float32
    )
    kx = (freq + qvec[0]) ** 2
    ky = (freq + qvec[1]) ** 2
    kz = (freq + qvec[2]) ** 2
    full = 4.0 / (kx[:, None, None] + ky[None, :, None] + kz[None, None, :] + 0.5)
    return full.reshape(count, count * count)


def apply_block(t_re, t_im, sources, kernel, forward_tab, inverse_tab, acc_re, acc_im):
    for member in range(sources.shape[0]):
        m_re = sources[member, 0].astype(jnp.float32)
        m_im = sources[member, 1].astype(jnp.float32)
        d_re = (m_re[None] * t_re + m_im[None] * t_im).astype(jnp.bfloat16)
        d_im = (m_re[None] * t_im - m_im[None] * t_re).astype(jnp.bfloat16)
        for target in range(t_re.shape[0]):
            density = jnp.stack([d_re[target], d_im[target]], axis=0)
            spectrum = transform(density, forward_tab)
            screened = (spectrum.astype(jnp.float32) * kernel[None]).astype(jnp.bfloat16)
            potential = transform(screened, inverse_tab).astype(jnp.float32)
            v_re = potential[0]
            v_im = potential[1]
            acc_re = acc_re.at[target].add(m_re * v_re - m_im * v_im)
            acc_im = acc_im.at[target].add(m_re * v_im + m_im * v_re)
    return (acc_re, acc_im)


def on_device(orbitals, kpoint_offsets, umklapp):
    local = orbitals[0]
    batch = local.shape[0]
    count = local.shape[2]
    kcount = kpoint_offsets.shape[0]
    forward_tab = section_table(count, False)
    inverse_tab = section_table(count, True)
    kidx = lax.axis_index("kpt")
    owner = lax.axis_size("band") // 2
    t_re = local[:, 0].astype(jnp.float32)
    t_im = local[:, 1].astype(jnp.float32)
    acc_re = jnp.zeros((batch, count, count * count), jnp.float32)
    acc_im = jnp.zeros((batch, count, count * count), jnp.float32)
    moving = local
    for step in range(KSTEPS):
        if step > 0:
            moving = from_behind(moving, "kpt", 1)
        received = from_root(moving, "band", owner)
        other = (kidx - step) % kcount
        mine = lax.dynamic_index_in_dim(kpoint_offsets, kidx, 0, False)
        theirs = lax.dynamic_index_in_dim(kpoint_offsets, other, 0, False)
        qvec = 0.5 * (mine - theirs).astype(jnp.float32) + umklapp[0, step].astype(jnp.float32)
        acc_re, acc_im = apply_block(
            t_re, t_im, received, screening(qvec, count), forward_tab, inverse_tab, acc_re, acc_im
        )
    merged = jnp.stack([-acc_re, -acc_im], axis=1)
    return merged.astype(jnp.bfloat16)[None]


def solution(mesh):
    return jax.shard_map(
        on_device,
        mesh=mesh,
        in_specs=(P("kpt", "band", None, None, None), P(), P("kpt", None, None)),
        out_specs=P("kpt", "band", None, None, None),
        check_vma=False,
    )
```

profile of v0, /device:TPU:1, one launch (start us, length us, event | category | flops | bytes accessed | tf_op | source)
XLA Modules:
  0.0 1219.7 jit_solution(5369295995786864034)
XLA Ops:
  6.5 4.0 collective-permute-start
  17.5 2.1 broadcast_select_fusion.1
  19.7 32.0 %collective-permute-done = bf16[2,2,48,2304]{3,2,1,0:T(8,128)(2,1)S(1)} collective-permute-done((bf16[2,2,48,2304]{3,2,1,0:T(8,128)(2,1)}, bf16[2,2,48,2304]{3,2,1,0:T(8,128)(2,1)S(1)}, u32[]{:S(2)}, u32[]{:S(2)}) %collective-permute-start) | collective-permute-done | bytes 884768 | tf_op jit(solution)/shard_map/ppermute | solution.py:13
  56.7 863.6 %all-reduce.3.cloned.1.call-done = (bf16[2,2,48,2304]{3,2,1,0:T(8,128)(2,1)}, bf16[2,2,48,2304]{3,2,1,0:T(8,128)(2,1)}) async-done(((bf16[2,2,48,2304]{3,2,1,0:T(8,128)(2,1)}, bf16[2,2,48,2304]{3,2,1,0:T(8,128)(2,1)}), (bf16[2,2,48,2304]{3,2,1,0:T(8,128)(2,1)}, bf16[2,2,48,2304]{3,2,1,0:T(8,128)(2,1)})) %all-reduce.3.cloned.1.call-update) | async-done | bytes 1769488 | tf_op jit(solution)/shard_map/psum | solution.py:18
  920.3 2.8 convert_bitcast_fusion.2
  923.1 1.8 fusion.37
  935.7 2.6 reshape.1122
  938.3 2.1 copy.46
  940.4 3.2 reshape.1098
  953.8 2.6 reshape.1121
  956.4 2.1 copy.39
  958.5 3.2 reshape.1096
  973.6 2.1 copy.32
  975.7 3.2 reshape.1092
  989.5 2.1 copy.25
  991.6 3.3 reshape.1090
  994.9 2.3 fusion.19
  1009.5 1.7 copy.28
  1026.6 1.7 copy.35
  1043.5 1.7 copy.42
  1060.5 1.7 copy.49
  1076.9 2.1 copy.74
  1079.0 3.2 reshape.1110
  1092.8 2.1 copy.67
  1094.9 3.3 reshape.1108
  1110.6 2.1 copy.60
  1112.7 3.2 reshape.1104
  1126.7 2.1 copy.53
  1128.9 3.3 reshape.1102
  1132.2 2.3 fusion.23
  1146.8 1.7 copy.56
  1163.8 1.7 copy.63
  (340 shorter events, 235.5 us)
Async XLA Ops:
  6.5 913.7 %all-reduce.3.cloned.1.call-start = ((), (), s32[]{:S(2)}) async-start(), calls=%async_computation | async-start | bytes 3538944 | tf_op jit(solution)/shard_map/psum | solution.py:18
  6.5 45.1 %collective-permute-start = (bf16[2,2,48,2304]{3,2,1,0:T(8,128)(2,1)}, bf16[2,2,48,2304]{3,2,1,0:T(8,128)(2,1)S(1)}, u32[]{:S(2)}, u32[]{:S(2)}) collective-permute-start(bf16[2,2,48,2304]{3,2,1,0:T(8,128)(2,1)} %bitcast.572), channel_id=1, source_target_pairs={{0,1},{1,2},{2,3},{3,4},{4,5},{5,6},{6,7},{7,0},{8,9},{9,10},{10,1... | collective-permute-start | bytes 2654216 | tf_op jit(solution)/shard_map/ppermute | solution.py:13
  920.3 2.8 copy-start
  940.4 3.2 copy-start.43
  958.5 3.2 copy-start.41
  958.5 3.2 copy-start.42
  975.7 3.2 copy-start.44
  991.6 3.3 copy-start.11
  991.6 3.3 copy-start.13
  991.6 3.3 copy-start.16
  991.6 3.3 copy-start.22
  1011.2 1.3 copy-start.3
  1028.3 1.3 copy-start.4
  1045.2 1.3 copy-start.5
  1062.3 1.3 copy-start.6
  1064.0 1.3 copy-start.20
  1079.0 3.2 copy-start.45
  1094.9 3.3 copy-start.19
  1112.7 3.2 copy-start.46
  1128.9 3.3 copy-start.12
  1128.9 3.3 copy-start.14
  1128.9 3.3 copy-start.15
  1128.9 3.3 copy-start.17
  1148.5 1.3 copy-start.7
  1165.5 1.3 copy-start.8
  1167.3 1.3 copy-start.26
  1182.7 1.3 copy-start.9
  1184.5 1.3 copy-start.24
  1199.7 1.3 copy-start.10
  1201.5 1.3 copy-start.40
  1206.6 1.3 copy-start.33
  1206.6 1.4 copy-start.34
  (17 other events, 19.3 us)
Sparse Core Ops, SparseCore 0:
  52.7 867.4 all-reduce.2
where the time goes:
time: 1230 us; the launch traced here: 1220 us
  waiting for transfers between devices  896 us (73%)
  local copies, waits for them, and re-layouts  266 us (22%)
  other arithmetic  24.8 us (2%)
  between operations  15 us (1%)
  matrix products  14.1 us (1%)
    psum x1, waiting for transfers between devices, from_root(): return lax.psum(jnp.where(mine, value, jnp.zeros_like(value)), axis)  864 us
    reshape x64, local copies, waits for them, and re-layouts, transform(): product.reshape(2, count, count, count).transpose(0, 2, 3, 1)  90.9 us
    convert_element_type x24, local copies, waits for them, and re-layouts, apply_block(): spectrum.astype(jnp.float32) * kernel[None]  56.6 us
    another operation x32, local copies, waits for them, and re-layouts, transform(): flat = parts.reshape(2 * count, count * count)  43.1 us
    slice x24, local copies, waits for them, and re-layouts, apply_block(): v_re = potential[0]  36.7 us
    ppermute x1, waiting for transfers between devices, from_behind(): lax.ppermute(value, axis, [(i, (i + by) % count) for i in range(count)])  32 us
  transfers between devices with their start and end apart: 2, of which 2 were waited for; matrix products, arithmetic and copies ran while one was open for 1% of the time, Pallas kernels for 0%

commit v1 on v0

v1 whole, which is shorter than its diff:
```python
import math

import jax
import jax.numpy as jnp
import numpy as np
from jax import lax
from jax.experimental import pallas as pl
from jax.experimental.pallas import tpu as pltpu
from jax.sharding import PartitionSpec as P

MESH = pl.DeviceIdType.MESH
KSTEPS = 2
RELAYS = (1, 4, 6)
HALF = 1152

G = 48
L = 128


def tables():
    idx = np.arange(G)
    ph = (idx[:, None] * idx[None, :] % G).astype(np.float32) * np.float32(2.0 * math.pi / G)
    scale = np.float32(1.0 / math.sqrt(G))
    c = (np.cos(ph) * scale).astype(np.float32)
    s = (np.sin(ph) * scale).astype(np.float32)
    right, left = [], []
    for sign in (1.0, -1.0):
        left.append(np.block([[c, sign * s], [-sign * s, c]]))
        big = np.zeros((256, 256), np.float32)
        for p in range(2):
            a = slice(p * G, p * G + G)
            b = slice(L + p * G, L + p * G + G)
            big[a, a] = c
            big[b, b] = c
            big[b, a] = sign * s
            big[a, b] = -sign * s
        right.append(big)
    return np.stack(left).astype(jnp.bfloat16), np.stack(right).astype(jnp.bfloat16)


def dot(a, b):
    return jnp.dot(a, b, preferred_element_type=jnp.float32)


def lanes():
    return lax.broadcasted_iota(jnp.int32, (G, L), 1)


def roll(v, s):
    s = s % L
    return v if s == 0 else pltpu.roll(v, s, 1)


def piece(tiles, j):
    o, t = (G * j) % L, (G * j) // L
    v = tiles[t]
    if o + G > L:
        v = jnp.where(lanes() >= o, v, tiles[t + 1])
    return v, o


def spread(tiles_a, tiles_b, j):
    a, o = piece(tiles_a, j)
    b, _ = piece(tiles_b, j)
    return jnp.where(lanes() < G, roll(a, -o), roll(b, G - o))


def load_tiles(ref, g, dt):
    base = g * 384 if isinstance(g, int) else pl.multiple_of(g * 384, 128)
    v = ref[:, pl.ds(base, 384)].astype(dt)
    return [v[:, i * L:(i + 1) * L] for i in range(3)]


def rows(i):
    if isinstance(i, int):
        return pl.ds(i * G, G)
    return pl.ds(pl.multiple_of(i * G, 16), G)


def relayout_targets(loc, tgt, dt):
    def body(g, _):
        for c in range(2):
            ta = load_tiles(loc.at[0, c], g, dt)
            tb = load_tiles(loc.at[1, c], g, dt)
            for j in range(8):
                tgt[c, rows(g * 8 + j), :] = spread(ta, tb, j).astype(jnp.bfloat16)
        return 0
    lax.fori_loop(0, 6, body, 0)


def make_kern(kern, s, q):
    def f(n):
        return ((n + G // 2) % G - G // 2).astype(jnp.float32)
    ly = lax.broadcasted_iota(jnp.int32, (G, L), 0)
    lz = lanes() % G
    yz = (f(ly) + q[1]) ** 2 + (f(lz) + q[2]) ** 2
    def body(x, _):
        kx = (f(x) + q[0]) ** 2
        kern[s, rows(x), :] = -4.0 / (kx + yz + 0.5)
        return 0
    lax.fori_loop(0, G, body, 0)


def pair_rhs(re0, re1, im0, im1):
    return jnp.concatenate(
        [jnp.concatenate([re0, re1], 1), jnp.concatenate([im0, im1], 1)], 0)


def phase_a(src, tgt, spr, b, left, right):
    bf = jnp.bfloat16
    rhs = []
    for g in range(6):
        tl = [load_tiles(src.at[c], g, bf) for c in range(2)]
        d = []
        for i in range(8):
            r = rows(g * 8 + i)
            m = [spread(tl[c], tl[c], i) for c in range(2)]
            spr[0, r, :] = m[0]
            spr[1, r, :] = m[1]
            mr, mi = m[0].astype(jnp.float32), m[1].astype(jnp.float32)
            tr, ti = tgt[0, r, :].astype(jnp.float32), tgt[1, r, :].astype(jnp.float32)
            d.append(jnp.concatenate([(mr * tr + mi * ti).astype(bf), (mr * ti - mi * tr).astype(bf)], 1))
        rhs.append(jnp.concatenate(d, 0))
    z = dot(jnp.concatenate(rhs, 0), right[0]).astype(bf)
    for y in range(0, G, 2):
        w = z[y * G:(y + 2) * G]
        o = dot(left[0], pair_rhs(w[:G, :L], w[G:, :L], w[:G, L:], w[G:, L:]))
        for i in range(2):
            for c in range(2):
                b[c, pl.ds(y + i, G, stride=G), :] = o[c * G:(c + 1) * G, i * L:(i + 1) * L]


def phase_b(b, cc, kern, left):
    bf = jnp.bfloat16
    for x in range(0, G, 2):
        v = [[b[c, rows(x + i), :].astype(bf) for i in range(2)] for c in range(2)]
        o = dot(left[0], pair_rhs(v[0][0], v[0][1], v[1][0], v[1][1]))
        k = jnp.concatenate([kern[rows(x), :], kern[rows(x + 1), :]], 1)
        o = dot(left[1], (o * jnp.concatenate([k, k], 0)).astype(bf))
        for i in range(2):
            for c in range(2):
                cc[c, pl.ds(x + i, G, stride=G), :] = o[c * G:(c + 1) * G, i * L:(i + 1) * L]


def phase_c(cc, spr, acc, left, right):
    bf = jnp.bfloat16
    n = 16
    def along_x(k):
        lhs = []
        for y in range(k * n, k * n + n, 2):
            v = [[cc[c, rows(y + i), :].astype(bf) for i in range(2)] for c in range(2)]
            o = dot(left[1], pair_rhs(v[0][0], v[0][1], v[1][0], v[1][1])).astype(bf)
            lhs += [jnp.concatenate([o[:G, :L], o[G:, :L]], 1), jnp.concatenate([o[:G, L:], o[G:, L:]], 1)]
        return jnp.concatenate(lhs, 0)
    lhs = along_x(0)
    for k in range(G // n):
        later = along_x(k + 1) if k + 1 < G // n else None
        p = dot(lhs, right[1])
        r = pl.ds(k * n * G, n * G)
        vr, vi = p[:, :L], p[:, L:]
        mr, mi = spr[0, r, :].astype(jnp.float32), spr[1, r, :].astype(jnp.float32)
        acc[0, r, :] += mr * vr - mi * vi
        acc[1, r, :] += mr * vi + mi * vr
        lhs = later


def gather_out(acc, out, dt):
    def body(g, _):
        ln = lanes()
        for c in range(2):
            a = [acc[c, rows(g * 8 + j), :].astype(dt) for j in range(8)]
            for p in range(2):
                tiles = [None] * 3
                for j in range(8):
                    o, t = (G * j) % L, (G * j) // L
                    r = roll(a[j], o - G * p)
                    tiles[t] = r if tiles[t] is None else jnp.where(ln >= o, r, tiles[t])
                    if o + G > L:
                        tiles[t + 1] = r
                base = pl.multiple_of(g * 384, 128)
                for t in range(3):
                    out[p, c, :, pl.ds(base + t * L, L)] = tiles[t].astype(jnp.bfloat16)
        return 0
    lax.fori_loop(0, 6, body, 0)


def share(loc, out, send, pieces, across, twin, sends):
    band, kpt = lax.axis_index("band"), lax.axis_index("kpt")
    nk = lax.axis_size("kpt")
    x, zl, core = band // 16, (band // 2) % 8, band % 2
    after, before = lax.rem(kpt + 1, nk), lax.rem(kpt + nk - 1, nk)
    root = 32
    is_root = band == root

    def at(bx, bz, bc):
        return bx * 16 + bz * 2 + bc

    def sites(ref, s, q, c, r):
        return ref.at[s, q // 2, c, pl.ds(r * 16, 16), pl.ds(pl.multiple_of((q % 2) * HALF, 128), HALF)]

    def xat(d):
        return lax.rem(x + d, 4)

    def scatter(s, q, r, c):
        return pltpu.make_async_remote_copy(
            src_ref=loc.at[q // 2, c, pl.ds(r * 16, 16), pl.ds((q % 2) * HALF, HALF)],
            dst_ref=sites(out, s, q, c, r),
            send_sem=send.at[s, q, r, c], recv_sem=pieces.at[s, r],
            device_id={"band": at(q, RELAYS[r], c), "kpt": kpt if s == 0 else after}, device_id_type=MESH)

    def column(s, r, d):
        return pltpu.make_async_remote_copy(
            src_ref=sites(out, s, x, core, r), dst_ref=sites(out, s, x, core, r),
            send_sem=sends.at[s, d - 1], recv_sem=pieces.at[s, r],
            device_id={"band": at(x, lax.rem(zl + d, 8), core), "kpt": kpt}, device_id_type=MESH)

    def row(s, r, d):
        return pltpu.make_async_remote_copy(
            src_ref=sites(out, s, x, core, r), dst_ref=sites(out, s, x, core, r),
            send_sem=sends.at[s, 7 + r * 3 + d - 1], recv_sem=across.at[s, r, d - 1],
            device_id={"band": at(xat(d), zl, core), "kpt": kpt}, device_id_type=MESH)

    def arrived(s, r, d):
        ref = sites(out, s, xat(4 - d), core, r)
        return pltpu.make_async_remote_copy(
            src_ref=ref, dst_ref=ref, send_sem=sends.at[s, 7 + r * 3 + d - 1], recv_sem=across.at[s, r, d - 1],
            device_id={"band": at(xat(d), zl, core), "kpt": kpt}, device_id_type=MESH)

    def to_twin(s, r, d, c):
        ref = sites(out, s, xat(4 - d) if d else x, c, r)
        return pltpu.make_async_remote_copy(
            src_ref=ref, dst_ref=ref, send_sem=sends.at[s, 16 + r * 4 + d], recv_sem=twin.at[s, r, d],
            device_id={"band": at(x, zl, 1 - core), "kpt": kpt}, device_id_type=MESH)

    relay = [zl == z for z in RELAYS]
    any_relay = relay[0] | relay[1] | relay[2]

    bar = pltpu.get_barrier_semaphore()

    def greet(b, k):
        pl.semaphore_signal(bar, inc=1, device_id={"band": b, "kpt": k}, device_id_type=MESH)

    @pl.when(any_relay)
    def _():
        greet(root, kpt)
        greet(root, before)

    for r in range(3):
        @pl.when(jnp.logical_not(relay[r]))
        def _():
            greet(at(x, RELAYS[r], core), kpt)
    for d in range(1, 4):
        greet(at(xat(d), zl, core), kpt)
    greet(at(x, zl, 1 - core), kpt)

    @pl.when(any_relay)
    def _():
        pl.semaphore_wait(bar, 11)

    @pl.when(jnp.logical_not(any_relay | is_root))
    def _():
        pl.semaphore_wait(bar, 4)

    @pl.when(is_root)
    def _():
        pl.semaphore_wait(bar, 52)
        for s in range(2):
            for r in range(3):
                for q in range(4):
                    for c in range(2):
                        scatter(s, q, r, c).start()

    def forward(s, r):
        column(s, r, 1).wait_recv()
        for d in range(1, 4):
            row(s, r, d).start()
        to_twin(s, r, 0, core).start()

    def lead(s):
        for r in range(3):
            @pl.when(relay[r])
            def _():
                column(s, r, 1).wait_recv()
                for d in range(1, 8):
                    column(s, r, d).start()
                for d in range(1, 4):
                    row(s, r, d).start()
                to_twin(s, r, 0, core).start()

    def rest(s):
        for r in range(3):
            @pl.when(jnp.logical_not(relay[r]))
            def _():
                forward(s, r)

    def take(s):
        for r in range(3):
            for d in (1, 3, 2):
                arrived(s, r, d).wait_recv()
                to_twin(s, r, d, core).start()

    def finish(s):
        for r in range(3):
            for d in range(4):
                to_twin(s, r, d, 1 - core).wait_recv()

    lead(0)
    rest(0)
    lead(1)
    take(0)
    rest(1)
    take(1)
    finish(0)
    finish(1)

    @pl.when(is_root)
    def _():
        for s in range(2):
            for r in range(3):
                for q in range(4):
                    for c in range(2):
                        scatter(s, q, r, c).wait_send()

    for s in range(2):
        @pl.when(any_relay)
        def _():
            for d in range(1, 8):
                column(s, 0, d).wait_send()
        for r in range(3):
            for d in range(1, 4):
                row(s, r, d).wait_send()
            for d in range(4):
                to_twin(s, r, d, core).wait_send()


def apply_all(koff, umk, loc, src, left, right, out, tgt, spr, b, cc, acc, kern):
    kpt = lax.axis_index("kpt")
    nk = lax.axis_size("kpt")
    relayout_targets(loc, tgt, jnp.bfloat16)
    for s in range(2):
        other = lax.rem(kpt + nk - s, nk)
        q = [0.5 * (koff[kpt, i] - koff[other, i]).astype(jnp.float32) + umk[s, i].astype(jnp.float32) for i in range(3)]
        make_kern(kern, s, q)
    acc[...] = jnp.zeros_like(acc)

    def one(u, _):
        phase_a(src.at[u // 2, u % 2], tgt, spr, b, left, right)
        phase_b(b, cc, kern.at[u // 2], left)
        phase_c(cc, spr, acc, left, right)
        return 0

    lax.fori_loop(0, 4, one, 0)
    gather_out(acc, out, jnp.float32)


def on_device(orbitals, koff, umklapp):
    bf = jnp.bfloat16
    loc = orbitals[0]
    left, right = tables()
    vmem = pl.BlockSpec(memory_space=pltpu.VMEM)
    smem = pl.BlockSpec(memory_space=pltpu.SMEM)
    src = pl.pallas_call(
        share,
        out_shape=jax.ShapeDtypeStruct((2,) + loc.shape, bf),
        in_specs=[vmem],
        out_specs=vmem,
        scratch_shapes=[
            pltpu.SemaphoreType.DMA((2, 4, 3, 2)),
            pltpu.SemaphoreType.DMA((2, 3)),
            pltpu.SemaphoreType.DMA((2, 3, 3)),
            pltpu.SemaphoreType.DMA((2, 3, 4)),
            pltpu.SemaphoreType.DMA((2, 28)),
        ],
        compiler_params=pltpu.CompilerParams(collective_id=0, has_side_effects=True, vmem_limit_bytes=32 * 2**20),
    )(loc)
    cube = (2, G * G, L)
    res = pl.pallas_call(
        apply_all,
        out_shape=jax.ShapeDtypeStruct(loc.shape, bf),
        in_specs=[smem, smem, vmem, vmem, vmem, vmem],
        out_specs=vmem,
        scratch_shapes=[pltpu.VMEM(cube, bf), pltpu.VMEM(cube, bf)] + [pltpu.VMEM(cube, jnp.float32)] * 4,
        compiler_params=pltpu.CompilerParams(vmem_limit_bytes=56 * 2**20),
    )(koff, umklapp[0], loc, src, jnp.asarray(left), jnp.asarray(right))
    return res[None]


def solution(mesh):
    return jax.shard_map(
        on_device,
        mesh=mesh,
        in_specs=(P("kpt", "band", None, None, None), P(), P("kpt", None, None)),
        out_specs=P("kpt", "band", None, None, None),
        check_vma=False,
    )
```

time: 1230 us -> 78.5 us (0.06)
  waiting for transfers between devices: 896 us -> 0 us
  local copies, waits for them, and re-layouts: 266 us -> 3.73 us
  Pallas kernels: 0 us -> 74.5 us
  other arithmetic: 24.8 us -> 0 us
  between operations: 15 us -> 0.02 us
  matrix products: 14.1 us -> 0 us
    psum x1 -> x0, waiting for transfers between devices: 864 us -> none  [from_root(): return lax.psum(jnp.where(mine, value, jnp.zeros_like(value)), axis)]
    reshape x64 -> x0, local copies, waits for them, and re-layouts: 90.9 us -> none  [transform(): product.reshape(2, count, count, count).transpose(0, 2, 3, 1)]
    pallas_call x0 -> x2, Pallas kernels: none -> 74.5 us  [the longest x1 52.7 us: on_device(): pl.pallas_call(share, out_shape=jax.ShapeDtypeStruct((2,) + loc.shape, bf...]
    convert_element_type x32 -> x0, local copies, waits for them, and re-layouts: 68.4 us -> none  [the longest x24 56.6 us: apply_block(): spectrum.astype(jnp.float32) * kernel[None]]
    slice x50 -> x0, local copies, waits for them, and re-layouts: 54.2 us -> none  [the longest x24 36.7 us: apply_block(): v_re = potential[0]]
    another operation x32 -> x0, local copies, waits for them, and re-layouts: 43.1 us -> none  [transform(): flat = parts.reshape(2 * count, count * count)]
    ppermute x1 -> x0, waiting for transfers between devices: 32 us -> none  [from_behind(): lax.ppermute(value, axis, [(i, (i + by) % count) for i in range(count)])]
    dot_general x48 -> x0, matrix products: 14.1 us -> none  [transform(): jnp.dot(table, flat, preferred_element_type=jnp.float32)]
  transfers between devices with their start and end apart: 2 -> 0, of which waited for: 2 -> 0; matrix products, arithmetic and copies ran while one was open for 1% -> 0% of each run, Pallas kernels for 0% -> 0%
where the time goes in v1:
time: 78.5 us; the launch traced here: 78.3 us
  Pallas kernels  74.5 us (95%)
  local copies, waits for them, and re-layouts  3.73 us (5%)
    pallas_call x1, Pallas kernels, on_device(): pl.pallas_call(share, out_shape=jax.ShapeDtypeStruct((2,) + loc.shape, bf...  52.7 us
    pallas_call x1, Pallas kernels, on_device(): pl.pallas_call(apply_all, out_shape=jax.ShapeDtypeStruct(loc.shape, bf),...  21.8 us
    unnamed x5, local copies, waits for them, and re-layouts  3.73 us

profile of v1, /device:TPU:1, one launch (start us, length us, event | category | flops | bytes accessed | tf_op | source)
XLA Modules:
  0.0 78.3 jit_solution(789797507180817380)
XLA Ops:
  0.0 1.3 %copy.6.koff = s32[8,3]{1,0:T(8,128)} copy(s32[8,3]{0,1:T(4,128)} %param.6) | data formatting | bytes 192 | tf_op args[1]
  1.3 0.0 copy-start.1
  1.4 1.2 %copy-done.1 = bf16[1,2,2,48,2304]{4,3,2,1,0:T(8,128)(2,1)S(1)} copy-done((bf16[1,2,2,48,2304]{4,3,2,1,0:T(8,128)(2,1)S(1)}, bf16[1,2,2,48,2304]{4,3,2,1,0:T(8,128)(2,1)}, u32[]{:S(2)}) %copy-start.1) | copy-done | bytes 884760
  2.5 52.7 %shard_map.55.src = bf16[2,2,2,48,2304]{4,3,2,1,0:T(8,128)(2,1)S(1)} custom-call(bf16[2,2,48,2304]{3,2,1,0:T(8,128)(2,1)S(1)} %bitcast.4), custom_call_target="tpu_custom_call" | custom-call | tf_op jit(solution)/shard_map/pallas_call | solution.py:362
  55.2 0.0 copy-start
  55.2 1.2 %copy-done = bf16[2,2,2,48,2304]{4,3,2,1,0:T(8,128)(2,1)} copy-done((bf16[2,2,2,48,2304]{4,3,2,1,0:T(8,128)(2,1)}, bf16[2,2,2,48,2304]{4,3,2,1,0:T(8,128)(2,1)S(1)}, u32[]{:S(2)}) %copy-start) | copy-done | bytes 1769496
  56.5 21.8 %shard_map.56 = bf16[2,2,48,2304]{3,2,1,0:T(8,128)(2,1)} custom-call(s32[8,3]{1,0:T(8,128)} %copy.6.koff, s32[2,3]{1,0:T(2,128)} %bitcast.5, bf16[2,2,48,2304]{3,2,1,0:T(8,128)(2,1)} %bitcast.3, bf16[2,2,2,48,2304]{4,3,2,1,0:T(8,128)(2,1)} %copy-done, bf16[2,96,96]{2,1,0:T(8,128)(2,1)} %constant.4.clone.left, bf16[2,256,256]{2,1,0:T(8,128)(2,1)} %constant.5.clone.right), custom_call_target="tpu_custom_call" | custom-call | tf_op jit(solution)/shard_map/pallas_call | solution.py:377
Async XLA Ops:
  1.3 1.2 %copy-start.1 = (bf16[1,2,2,48,2304]{4,3,2,1,0:T(8,128)(2,1)S(1)}, bf16[1,2,2,48,2304]{4,3,2,1,0:T(8,128)(2,1)}, u32[]{:S(2)}) copy-start(bf16[1,2,2,48,2304]{4,3,2,1,0:T(8,128)(2,1)} %param.5) | copy-start | bytes 2654212
  55.2 1.2 %copy-start = (bf16[2,2,2,48,2304]{4,3,2,1,0:T(8,128)(2,1)}, bf16[2,2,2,48,2304]{4,3,2,1,0:T(8,128)(2,1)S(1)}, u32[]{:S(2)}) copy-start(bf16[2,2,2,48,2304]{4,3,2,1,0:T(8,128)(2,1)S(1)} %shard_map.55.src) | copy-start | bytes 5308420

commit v2 on v1

--- a/solution.py
+++ b/solution.py
@@ -10,8 +10,10 @@
 
 MESH = pl.DeviceIdType.MESH
 KSTEPS = 2
-RELAYS = (1, 4, 6)
+RELAYS = (6, 4, 1)
 HALF = 1152
+ROOT = 32
+SEEDS = ((2, 0), (3, 1)), ((1, 0), (0, 1))
 
 G = 48
 L = 128
@@ -184,95 +186,135 @@
     lax.fori_loop(0, 6, body, 0)
 
 
-def share(loc, out, send, pieces, across, twin, sends):
+def kernel(loc, koff, umk, left_in, right_in, out, src, tgt, spr, b, cc, acc, kern, mine, left, right, held, ks, us,
+           local, first, seeded, seed_send, pieces, across, twin, sends):
     band, kpt = lax.axis_index("band"), lax.axis_index("kpt")
     nk = lax.axis_size("kpt")
     x, zl, core = band // 16, (band // 2) % 8, band % 2
     after, before = lax.rem(kpt + 1, nk), lax.rem(kpt + nk - 1, nk)
-    root = 32
-    is_root = band == root
+    is_root = band == ROOT
 
     def at(bx, bz, bc):
         return bx * 16 + bz * 2 + bc
 
-    def sites(ref, s, q, c, r):
-        return ref.at[s, q // 2, c, pl.ds(r * 16, 16), pl.ds(pl.multiple_of((q % 2) * HALF, 128), HALF)]
-
     def xat(d):
         return lax.rem(x + d, 4)
 
-    def scatter(s, q, r, c):
+    def site(s, u, q, r):
+        return src.at[s, u, q // 2, pl.ds(r * 16, 16), pl.ds(pl.multiple_of((q % 2) * HALF, 128), HALF)]
+
+    def held_piece(q, r):
+        return held.at[q // 2, pl.ds(r * 16, 16), pl.ds((q % 2) * HALF, HALF)]
+
+    def remote(source, target, send, recv, b_, k_=kpt):
         return pltpu.make_async_remote_copy(
-            src_ref=loc.at[q // 2, c, pl.ds(r * 16, 16), pl.ds((q % 2) * HALF, HALF)],
-            dst_ref=sites(out, s, q, c, r),
-            send_sem=send.at[s, q, r, c], recv_sem=pieces.at[s, r],
-            device_id={"band": at(q, RELAYS[r], c), "kpt": kpt if s == 0 else after}, device_id_type=MESH)
+            src_ref=source, dst_ref=target, send_sem=send, recv_sem=recv,
+            device_id={"band": b_, "kpt": k_}, device_id_type=MESH)
+
+    def from_root(s, u, q, r):
+        own = s == 0 and u == 0
+        target = site(s, u, q, r) if own else held_piece(q, r)
+        to = at(q, RELAYS[r], 0) if own else at(SEEDS[s][u][0], 0, u)
+        return remote(
+            loc.at[u, q // 2, pl.ds(r * 16, 16), pl.ds((q % 2) * HALF, HALF)], target,
+            first.at[s * 2 + u, q, r], pieces.at[s, r] if own else seeded.at[q, r], to, kpt if s == 0 else after)
+
+    def from_seed(s, u, q, r):
+        return remote(held_piece(q, r), site(s, u, q, r), seed_send.at[q, r], pieces.at[s, r], at(q, RELAYS[r], u))
 
     def column(s, r, d):
-        return pltpu.make_async_remote_copy(
-            src_ref=sites(out, s, x, core, r), dst_ref=sites(out, s, x, core, r),
-            send_sem=sends.at[s, d - 1], recv_sem=pieces.at[s, r],
-            device_id={"band": at(x, lax.rem(zl + d, 8), core), "kpt": kpt}, device_id_type=MESH)
+        ref = site(s, core, x, r)
+        return remote(ref, ref, sends.at[s, d - 1], pieces.at[s, r], at(x, lax.rem(zl + d, 8), core))
 
     def row(s, r, d):
-        return pltpu.make_async_remote_copy(
-            src_ref=sites(out, s, x, core, r), dst_ref=sites(out, s, x, core, r),
-            send_sem=sends.at[s, 7 + r * 3 + d - 1], recv_sem=across.at[s, r, d - 1],
-            device_id={"band": at(xat(d), zl, core), "kpt": kpt}, device_id_type=MESH)
+        ref = site(s, core, x, r)
+        return remote(ref, ref, sends.at[s, 7 + r * 3 + d - 1], across.at[s, r, d - 1], at(xat(d), zl, core))
 
     def arrived(s, r, d):
-        ref = sites(out, s, xat(4 - d), core, r)
-        return pltpu.make_async_remote_copy(
-            src_ref=ref, dst_ref=ref, send_sem=sends.at[s, 7 + r * 3 + d - 1], recv_sem=across.at[s, r, d - 1],
-            device_id={"band": at(xat(d), zl, core), "kpt": kpt}, device_id_type=MESH)
-
-    def to_twin(s, r, d, c):
-        ref = sites(out, s, xat(4 - d) if d else x, c, r)
-        return pltpu.make_async_remote_copy(
-            src_ref=ref, dst_ref=ref, send_sem=sends.at[s, 16 + r * 4 + d], recv_sem=twin.at[s, r, d],
-            device_id={"band": at(x, zl, 1 - core), "kpt": kpt}, device_id_type=MESH)
+        ref = site(s, core, xat(4 - d), r)
+        return remote(ref, ref, sends.at[s, 7 + r * 3 + d - 1], across.at[s, r, d - 1], at(xat(d), zl, core))
+
+    def to_twin(s, r, d, u):
+        ref = site(s, u, xat(4 - d) if d else x, r)
+        return remote(ref, ref, sends.at[s, 16 + r * 4 + d], twin.at[s, r, d], at(x, zl, 1 - core))
 
     relay = [zl == z for z in RELAYS]
     any_relay = relay[0] | relay[1] | relay[2]
+    seeds = [(s, u, (x == SEEDS[s][u][0]) & (zl == 0) & (core == u)) for s, u in ((0, 1), (1, 0), (1, 1))]
+    any_seed = seeds[0][2] | seeds[1][2] | seeds[2][2]
 
     bar = pltpu.get_barrier_semaphore()
 
-    def greet(b, k):
-        pl.semaphore_signal(bar, inc=1, device_id={"band": b, "kpt": k}, device_id_type=MESH)
+    def greet(b_, k_=kpt):
+        pl.semaphore_signal(bar, inc=1, device_id={"band": b_, "kpt": k_}, device_id_type=MESH)
 
     @pl.when(any_relay)
     def _():
-        greet(root, kpt)
-        greet(root, before)
+        for s in range(2):
+            greet(jnp.where(core == 0, at(SEEDS[s][0][0], 0, 0), at(SEEDS[s][1][0], 0, 1)))
+
+    for s, u, here in seeds:
+        @pl.when(here)
+        def _():
+            greet(ROOT, kpt if s == 0 else before)
 
     for r in range(3):
         @pl.when(jnp.logical_not(relay[r]))
         def _():
-            greet(at(x, RELAYS[r], core), kpt)
+            greet(at(x, RELAYS[r], core))
     for d in range(1, 4):
-        greet(at(xat(d), zl, core), kpt)
-    greet(at(x, zl, 1 - core), kpt)
+        greet(at(xat(d), zl, core))
+    greet(at(x, zl, 1 - core))
+
+    copies = [pltpu.make_async_copy(a, c, local.at[i]) for i, (a, c) in enumerate(
+        ((loc, mine), (left_in, left), (right_in, right), (koff, ks), (umk, us)))]
+    for c in copies:
+        c.start()
 
     @pl.when(any_relay)
     def _():
         pl.semaphore_wait(bar, 11)
 
-    @pl.when(jnp.logical_not(any_relay | is_root))
+    @pl.when(any_seed)
+    def _():
+        pl.semaphore_wait(bar, 16)
+
+    @pl.when(is_root)
+    def _():
+        pl.semaphore_wait(bar, 19)
+
+    @pl.when(jnp.logical_not(any_relay | any_seed | is_root))
     def _():
         pl.semaphore_wait(bar, 4)
 
+    def each_piece(f):
+        for r in range(3):
+            for q in range(4):
+                f(q, r)
+
     @pl.when(is_root)
     def _():
-        pl.semaphore_wait(bar, 52)
-        for s in range(2):
-            for r in range(3):
-                for q in range(4):
-                    for c in range(2):
-                        scatter(s, q, r, c).start()
-
-    def forward(s, r):
-        column(s, r, 1).wait_recv()
-        for d in range(1, 4):
+        each_piece(lambda q, r: [from_root(s, u, q, r).start() for s, u in ((0, 0), (0, 1))])
+        each_piece(lambda q, r: [from_root(s, u, q, r).start() for s, u in ((1, 0), (1, 1))])
+
+    for c in copies:
+        c.wait()
+    relayout_targets(mine, tgt, jnp.bfloat16)
+    for s in range(2):
+        other = lax.rem(kpt + nk - s, nk)
+        make_kern(kern, s, [0.5 * (ks[i, kpt] - ks[i, other]).astype(jnp.float32) + us[s, i].astype(jnp.float32) for i in range(3)])
+    acc[...] = jnp.zeros_like(acc)
+
+    for s, u, here in seeds:
+        @pl.when(here)
+        def _():
+            def pass_on(q, r):
+                from_root(s, u, q, r).wait_recv()
+                from_seed(s, u, q, r).start()
+            each_piece(pass_on)
+
+    def spread_piece(s, r):
+        for d in (2, 1, 3):
             row(s, r, d).start()
         to_twin(s, r, 0, core).start()
 
@@ -283,15 +325,14 @@
                 column(s, r, 1).wait_recv()
                 for d in range(1, 8):
                     column(s, r, d).start()
-                for d in range(1, 4):
-                    row(s, r, d).start()
-                to_twin(s, r, 0, core).start()
+                spread_piece(s, r)
 
     def rest(s):
         for r in range(3):
             @pl.when(jnp.logical_not(relay[r]))
             def _():
-                forward(s, r)
+                column(s, r, 1).wait_recv()
+                spread_piece(s, r)
 
     def take(s):
         for r in range(3):
@@ -308,18 +349,43 @@
     rest(0)
     lead(1)
     take(0)
-    rest(1)
-    take(1)
-    finish(0)
-    finish(1)
+
+    def one(u, _):
+        m = lax.rem(core + u, 2)
+
+        @pl.when(u == 1)
+        def _():
+            finish(0)
+
+        @pl.when(u == 3)
+        def _():
+            finish(1)
+
+        phase_a(src.at[u // 2, m], tgt, spr, b, left, right)
+
+        @pl.when(u == 0)
+        def _():
+            rest(1)
+
+        phase_b(b, cc, kern.at[u // 2], left)
+
+        @pl.when(u == 1)
+        def _():
+            take(1)
+
+        phase_c(cc, spr, acc, left, right)
+        return 0
+
+    lax.fori_loop(0, 4, one, 0)
+    gather_out(acc, out, jnp.float32)
 
     @pl.when(is_root)
     def _():
-        for s in range(2):
-            for r in range(3):
-                for q in range(4):
-                    for c in range(2):
-                        scatter(s, q, r, c).wait_send()
+        each_piece(lambda q, r: [from_root(s, u, q, r).wait_send() for s in range(2) for u in range(2)])
+
+    @pl.when(any_seed)
+    def _():
+        each_piece(lambda q, r: from_seed(0, 1, q, r).wait_send())
 
     for s in range(2):
         @pl.when(any_relay)
@@ -333,55 +399,25 @@
                 to_twin(s, r, d, core).wait_send()
 
 
-def apply_all(koff, umk, loc, src, left, right, out, tgt, spr, b, cc, acc, kern):
-    kpt = lax.axis_index("kpt")
-    nk = lax.axis_size("kpt")
-    relayout_targets(loc, tgt, jnp.bfloat16)
-    for s in range(2):
-        other = lax.rem(kpt + nk - s, nk)
-        q = [0.5 * (koff[kpt, i] - koff[other, i]).astype(jnp.float32) + umk[s, i].astype(jnp.float32) for i in range(3)]
-        make_kern(kern, s, q)
-    acc[...] = jnp.zeros_like(acc)
-
-    def one(u, _):
-        phase_a(src.at[u // 2, u % 2], tgt, spr, b, left, right)
-        phase_b(b, cc, kern.at[u // 2], left)
-        phase_c(cc, spr, acc, left, right)
-        return 0
-
-    lax.fori_loop(0, 4, one, 0)
-    gather_out(acc, out, jnp.float32)
-
-
 def on_device(orbitals, koff, umklapp):
     bf = jnp.bfloat16
     loc = orbitals[0]
     left, right = tables()
-    vmem = pl.BlockSpec(memory_space=pltpu.VMEM)
-    smem = pl.BlockSpec(memory_space=pltpu.SMEM)
-    src = pl.pallas_call(
-        share,
-        out_shape=jax.ShapeDtypeStruct((2,) + loc.shape, bf),
-        in_specs=[vmem],
-        out_specs=vmem,
-        scratch_shapes=[
-            pltpu.SemaphoreType.DMA((2, 4, 3, 2)),
-            pltpu.SemaphoreType.DMA((2, 3)),
-            pltpu.SemaphoreType.DMA((2, 3, 3)),
-            pltpu.SemaphoreType.DMA((2, 3, 4)),
-            pltpu.SemaphoreType.DMA((2, 28)),
-        ],
-        compiler_params=pltpu.CompilerParams(collective_id=0, has_side_effects=True, vmem_limit_bytes=32 * 2**20),
-    )(loc)
+    hbm = pl.BlockSpec(memory_space=pl.ANY)
+    dma = pltpu.SemaphoreType.DMA
     cube = (2, G * G, L)
     res = pl.pallas_call(
-        apply_all,
+        kernel,
         out_shape=jax.ShapeDtypeStruct(loc.shape, bf),
-        in_specs=[smem, smem, vmem, vmem, vmem, vmem],
-        out_specs=vmem,
-        scratch_shapes=[pltpu.VMEM(cube, bf), pltpu.VMEM(cube, bf)] + [pltpu.VMEM(cube, jnp.float32)] * 4,
-        compiler_params=pltpu.CompilerParams(vmem_limit_bytes=56 * 2**20),
-    )(koff, umklapp[0], loc, src, jnp.asarray(left), jnp.asarray(right))
+        in_specs=[hbm] * 5,
+        out_specs=pl.BlockSpec(memory_space=pltpu.VMEM),
+        scratch_shapes=[pltpu.VMEM((2,) + loc.shape, bf), pltpu.VMEM(cube, bf), pltpu.VMEM(cube, bf)]
+        + [pltpu.VMEM(cube, jnp.float32)] * 4
+        + [pltpu.VMEM(loc.shape, bf), pltpu.VMEM(left.shape, bf), pltpu.VMEM(right.shape, bf), pltpu.VMEM(loc.shape[1:], bf)]
+        + [pltpu.SMEM((3, koff.shape[0]), jnp.int32), pltpu.SMEM(umklapp.shape[1:], jnp.int32)]
+        + [dma((5,)), dma((4, 4, 3)), dma((4, 3)), dma((4, 3)), dma((2, 3)), dma((2, 3, 3)), dma((2, 3, 4)), dma((2, 28))],
+        compiler_params=pltpu.CompilerParams(collective_id=0, has_side_effects=True, vmem_limit_bytes=56 * 2**20),
+    )(loc, koff.T, umklapp[0], jnp.asarray(left), jnp.asarray(right))
     return res[None]
 
 

time: 78.5 us -> 68 us (0.87)
  Pallas kernels: 74.5 us -> 65.7 us
  local copies, waits for them, and re-layouts: 3.73 us -> 2.14 us
    pallas_call x2 -> x1, Pallas kernels: 74.5 us -> 65.7 us  [on_device(): pl.pallas_call(kernel, out_shape=jax.ShapeDtypeStruct(loc.shape, bf), in_...]
    unnamed x5 -> x1, local copies, waits for them, and re-layouts: 3.73 us -> 2.14 us
where the time goes in v2:
time: 68 us; the launch traced here: 67.8 us
  Pallas kernels  65.7 us (97%)
  local copies, waits for them, and re-layouts  2.14 us (3%)
    pallas_call x1, Pallas kernels, on_device(): pl.pallas_call(kernel, out_shape=jax.ShapeDtypeStruct(loc.shape, bf), in_...  65.7 us
    unnamed x1, local copies, waits for them, and re-layouts  2.14 us

profile of v2, /device:TPU:1, one launch (start us, length us, event | category | flops | bytes accessed | tf_op | source)
XLA Modules:
  0.0 67.8 jit_solution(16947405453323389827)
XLA Ops:
  0.0 65.7 %shard_map.55 = bf16[2,2,48,2304]{3,2,1,0:T(8,128)(2,1)} custom-call(bf16[2,2,48,2304]{3,2,1,0:T(8,128)(2,1)} %bitcast.5, s32[3,8]{1,0:T(4,128)} %bitcast.6, s32[2,3]{1,0:T(2,128)} %bitcast.7, bf16[2,96,96]{2,1,0:T(8,128)(2,1)} %constant.4.clone.left_in, bf16[2,256,256]{2,1,0:T(8,128)(2,1)} %constant.5.clone.right_in), custom_call_target="tpu_custom_call" | custom-call | tf_op jit(solution)/shard_map/pallas_call | solution.py:409
  65.7 2.1 %copy.7 = bf16[1,2,2,48,2304]{4,3,2,1,0:T(8,128)(2,1)} copy(bf16[1,2,2,48,2304]{4,3,2,1,0:T(8,128)(2,1)} %bitcast.4) | data formatting | bytes 1769472

commit v3 on v2

--- a/solution.py
+++ b/solution.py
@@ -214,7 +214,7 @@
     def from_root(s, u, q, r):
         own = s == 0 and u == 0
         target = site(s, u, q, r) if own else held_piece(q, r)
-        to = at(q, RELAYS[r], 0) if own else at(SEEDS[s][u][0], 0, u)
+        to = at(q, RELAYS[r], 0) if own else at(SEEDS[s][u][0], seed_z(s, after), u)
         return remote(
             loc.at[u, q // 2, pl.ds(r * 16, 16), pl.ds((q % 2) * HALF, HALF)], target,
             first.at[s * 2 + u, q, r], pieces.at[s, r] if own else seeded.at[q, r], to, kpt if s == 0 else after)
@@ -238,9 +238,12 @@
         ref = site(s, u, xat(4 - d) if d else x, r)
         return remote(ref, ref, sends.at[s, 16 + r * 4 + d], twin.at[s, r, d], at(x, zl, 1 - core))
 
+    def seed_z(s, k):
+        return jnp.where(lax.rem(k, 4) == 0, 7, 0) if s else 0
+
     relay = [zl == z for z in RELAYS]
     any_relay = relay[0] | relay[1] | relay[2]
-    seeds = [(s, u, (x == SEEDS[s][u][0]) & (zl == 0) & (core == u)) for s, u in ((0, 1), (1, 0), (1, 1))]
+    seeds = [(s, u, (x == SEEDS[s][u][0]) & (zl == seed_z(s, kpt)) & (core == u)) for s, u in ((0, 1), (1, 0), (1, 1))]
     any_seed = seeds[0][2] | seeds[1][2] | seeds[2][2]
 
     bar = pltpu.get_barrier_semaphore()
@@ -251,7 +254,7 @@
     @pl.when(any_relay)
     def _():
         for s in range(2):
-            greet(jnp.where(core == 0, at(SEEDS[s][0][0], 0, 0), at(SEEDS[s][1][0], 0, 1)))
+            greet(jnp.where(core == 0, at(SEEDS[s][0][0], seed_z(s, kpt), 0), at(SEEDS[s][1][0], seed_z(s, kpt), 1)))
 
     for s, u, here in seeds:
         @pl.when(here)

time: 68 us -> 58.5 us (0.86); the launches traced: 67.8 us -> 57.6 us
  Pallas kernels: 65.7 us -> 55.5 us
    pallas_call x1, Pallas kernels: 65.7 us -> 55.5 us  [on_device(): pl.pallas_call(kernel, out_shape=jax.ShapeDtypeStruct(loc.shape, bf), in_...]
where the time goes in v3:
time: 58.5 us; the launch traced here: 57.6 us
  Pallas kernels  55.5 us (95%)
  local copies, waits for them, and re-layouts  2.14 us (4%)
    pallas_call x1, Pallas kernels, on_device(): pl.pallas_call(kernel, out_shape=jax.ShapeDtypeStruct(loc.shape, bf), in_...  55.5 us
    unnamed x1, local copies, waits for them, and re-layouts  2.14 us

profile of v3, /device:TPU:1, one launch (start us, length us, event | category | flops | bytes accessed | tf_op | source)
XLA Modules:
  0.0 57.6 jit_solution(1943351587648990564)
XLA Ops:
  0.0 55.5 %shard_map.55 = bf16[2,2,48,2304]{3,2,1,0:T(8,128)(2,1)} custom-call(bf16[2,2,48,2304]{3,2,1,0:T(8,128)(2,1)} %bitcast.5, s32[3,8]{1,0:T(4,128)} %bitcast.6, s32[2,3]{1,0:T(2,128)} %bitcast.7, bf16[2,96,96]{2,1,0:T(8,128)(2,1)} %constant.4.clone.left_in, bf16[2,256,256]{2,1,0:T(8,128)(2,1)} %constant.5.clone.right_in), custom_call_target="tpu_custom_call" | custom-call | tf_op jit(solution)/shard_map/pallas_call | solution.py:412
  55.5 2.1 %copy.7 = bf16[1,2,2,48,2304]{4,3,2,1,0:T(8,128)(2,1)} copy(bf16[1,2,2,48,2304]{4,3,2,1,0:T(8,128)(2,1)} %bitcast.4) | data formatting | bytes 1769472

commit v4 on v3

--- a/solution.py
+++ b/solution.py
@@ -10,7 +10,7 @@
 
 MESH = pl.DeviceIdType.MESH
 KSTEPS = 2
-RELAYS = (6, 4, 1)
+RELAYS = (3, 2, 1)
 HALF = 1152
 ROOT = 32
 SEEDS = ((2, 0), (3, 1)), ((1, 0), (0, 1))
@@ -214,13 +214,13 @@
     def from_root(s, u, q, r):
         own = s == 0 and u == 0
         target = site(s, u, q, r) if own else held_piece(q, r)
-        to = at(q, RELAYS[r], 0) if own else at(SEEDS[s][u][0], seed_z(s, after), u)
+        to = at(q, place(s, r, kpt), 0) if own else at(SEEDS[s][u][0], seed_z(s, after), u)
         return remote(
             loc.at[u, q // 2, pl.ds(r * 16, 16), pl.ds((q % 2) * HALF, HALF)], target,
             first.at[s * 2 + u, q, r], pieces.at[s, r] if own else seeded.at[q, r], to, kpt if s == 0 else after)
 
     def from_seed(s, u, q, r):
-        return remote(held_piece(q, r), site(s, u, q, r), seed_send.at[q, r], pieces.at[s, r], at(q, RELAYS[r], u))
+        return remote(held_piece(q, r), site(s, u, q, r), seed_send.at[q, r], pieces.at[s, r], at(q, place(s, r, kpt), u))
 
     def column(s, r, d):
         ref = site(s, core, x, r)
@@ -241,8 +241,11 @@
     def seed_z(s, k):
         return jnp.where(lax.rem(k, 4) == 0, 7, 0) if s else 0
 
-    relay = [zl == z for z in RELAYS]
-    any_relay = relay[0] | relay[1] | relay[2]
+    def place(s, r, k):
+        return jnp.where(seed_z(s, k) == 7, 7 - RELAYS[r], RELAYS[r])
+
+    relay = [[zl == place(s, r, kpt) for r in range(3)] for s in range(2)]
+    any_relay = [relay[s][0] | relay[s][1] | relay[s][2] for s in range(2)]
     seeds = [(s, u, (x == SEEDS[s][u][0]) & (zl == seed_z(s, kpt)) & (core == u)) for s, u in ((0, 1), (1, 0), (1, 1))]
     any_seed = seeds[0][2] | seeds[1][2] | seeds[2][2]
 
@@ -251,9 +254,9 @@
     def greet(b_, k_=kpt):
         pl.semaphore_signal(bar, inc=1, device_id={"band": b_, "kpt": k_}, device_id_type=MESH)
 
-    @pl.when(any_relay)
-    def _():
-        for s in range(2):
+    for s in range(2):
+        @pl.when(any_relay[s])
+        def _():
             greet(jnp.where(core == 0, at(SEEDS[s][0][0], seed_z(s, kpt), 0), at(SEEDS[s][1][0], seed_z(s, kpt), 1)))
 
     for s, u, here in seeds:
@@ -261,10 +264,11 @@
         def _():
             greet(ROOT, kpt if s == 0 else before)
 
-    for r in range(3):
-        @pl.when(jnp.logical_not(relay[r]))
-        def _():
-            greet(at(x, RELAYS[r], core))
+    for s in range(2):
+        for r in range(3):
+            @pl.when(jnp.logical_not(relay[s][r]))
+            def _():
+                greet(at(x, place(s, r, kpt), core))
     for d in range(1, 4):
         greet(at(xat(d), zl, core))
     greet(at(x, zl, 1 - core))
@@ -274,10 +278,14 @@
     for c in copies:
         c.start()
 
-    @pl.when(any_relay)
+    @pl.when(any_relay[0] ^ any_relay[1])
     def _():
         pl.semaphore_wait(bar, 11)
 
+    @pl.when(any_relay[0] & any_relay[1])
+    def _():
+        pl.semaphore_wait(bar, 18)
+
     @pl.when(any_seed)
     def _():
         pl.semaphore_wait(bar, 16)
@@ -286,7 +294,7 @@
     def _():
         pl.semaphore_wait(bar, 19)
 
-    @pl.when(jnp.logical_not(any_relay | any_seed | is_root))
+    @pl.when(jnp.logical_not(any_relay[0] | any_relay[1] | any_seed | is_root))
     def _():
         pl.semaphore_wait(bar, 4)
 
@@ -323,7 +331,7 @@
 
     def lead(s):
         for r in range(3):
-            @pl.when(relay[r])
+            @pl.when(relay[s][r])
             def _():
                 column(s, r, 1).wait_recv()
                 for d in range(1, 8):
@@ -332,7 +340,7 @@
 
     def rest(s):
         for r in range(3):
-            @pl.when(jnp.logical_not(relay[r]))
+            @pl.when(jnp.logical_not(relay[s][r]))
             def _():
                 column(s, r, 1).wait_recv()
                 spread_piece(s, r)
@@ -391,7 +399,7 @@
         each_piece(lambda q, r: from_seed(0, 1, q, r).wait_send())
 
     for s in range(2):
-        @pl.when(any_relay)
+        @pl.when(any_relay[s])
         def _():
             for d in range(1, 8):
                 column(s, 0, d).wait_send()

time: 58.5 us -> 57.3 us (0.979)
  the two profiles are of different devices: /device:TPU:1 before, /device:TPU:6 now
where the time goes in v4:
time: 57.3 us; the launch traced here: 57.1 us
  Pallas kernels  54.9 us (96%)
  local copies, waits for them, and re-layouts  2.14 us (4%)
    pallas_call x1, Pallas kernels, on_device(): pl.pallas_call(kernel, out_shape=jax.ShapeDtypeStruct(loc.shape, bf), in_...  54.9 us
    unnamed x1, local copies, waits for them, and re-layouts  2.14 us

profile of v4, /device:TPU:6, one launch (start us, length us, event | category | flops | bytes accessed | tf_op | source)
XLA Modules:
  0.0 57.1 jit_solution(9398931061850339681)
XLA Ops:
  0.0 54.9 %shard_map.55 = bf16[2,2,48,2304]{3,2,1,0:T(8,128)(2,1)} custom-call(bf16[2,2,48,2304]{3,2,1,0:T(8,128)(2,1)} %bitcast.5, s32[3,8]{1,0:T(4,128)} %bitcast.6, s32[2,3]{1,0:T(2,128)} %bitcast.7, bf16[2,96,96]{2,1,0:T(8,128)(2,1)} %constant.4.clone.left_in, bf16[2,256,256]{2,1,0:T(8,128)(2,1)} %constant.5.clone.right_in), custom_call_target="tpu_custom_call" | custom-call | tf_op jit(solution)/shard_map/pallas_call | solution.py:420
  54.9 2.1 %copy.7 = bf16[1,2,2,48,2304]{4,3,2,1,0:T(8,128)(2,1)} copy(bf16[1,2,2,48,2304]{4,3,2,1,0:T(8,128)(2,1)} %bitcast.4) | data formatting | bytes 1769472

commit v5 on v4

--- a/solution.py
+++ b/solution.py
@@ -10,7 +10,7 @@
 
 MESH = pl.DeviceIdType.MESH
 KSTEPS = 2
-RELAYS = (3, 2, 1)
+RELAYS = (5, 3, 1)
 HALF = 1152
 ROOT = 32
 SEEDS = ((2, 0), (3, 1)), ((1, 0), (0, 1))
@@ -219,6 +219,11 @@
             loc.at[u, q // 2, pl.ds(r * 16, 16), pl.ds((q % 2) * HALF, HALF)], target,
             first.at[s * 2 + u, q, r], pieces.at[s, r] if own else seeded.at[q, r], to, kpt if s == 0 else after)
 
+    def onward(q, r):
+        return remote(
+            held_piece(q, r), held_piece(q, r), first.at[3, q, r], seeded.at[q, r],
+            at(SEEDS[1][1][0], seed_z(1, after), 1), after)
+
     def from_seed(s, u, q, r):
         return remote(held_piece(q, r), site(s, u, q, r), seed_send.at[q, r], pieces.at[s, r], at(q, place(s, r, kpt), u))
 
@@ -262,7 +267,7 @@
     for s, u, here in seeds:
         @pl.when(here)
         def _():
-            greet(ROOT, kpt if s == 0 else before)
+            greet(at(SEEDS[0][1][0], 0, 1) if s and u else ROOT, before if s else kpt)
 
     for s in range(2):
         for r in range(3):
@@ -286,13 +291,17 @@
     def _():
         pl.semaphore_wait(bar, 18)
 
-    @pl.when(any_seed)
+    @pl.when(seeds[0][2])
+    def _():
+        pl.semaphore_wait(bar, 17)
+
+    @pl.when(seeds[1][2] | seeds[2][2])
     def _():
         pl.semaphore_wait(bar, 16)
 
     @pl.when(is_root)
     def _():
-        pl.semaphore_wait(bar, 19)
+        pl.semaphore_wait(bar, 18)
 
     @pl.when(jnp.logical_not(any_relay[0] | any_relay[1] | any_seed | is_root))
     def _():
@@ -305,8 +314,7 @@
 
     @pl.when(is_root)
     def _():
-        each_piece(lambda q, r: [from_root(s, u, q, r).start() for s, u in ((0, 0), (0, 1))])
-        each_piece(lambda q, r: [from_root(s, u, q, r).start() for s, u in ((1, 0), (1, 1))])
+        each_piece(lambda q, r: [from_root(s, u, q, r).start() for s, u in ((0, 1), (0, 0), (1, 0))])
 
     for c in copies:
         c.wait()
@@ -322,6 +330,8 @@
             def pass_on(q, r):
                 from_root(s, u, q, r).wait_recv()
                 from_seed(s, u, q, r).start()
+                if s == 0:
+                    onward(q, r).start()
             each_piece(pass_on)
 
     def spread_piece(s, r):
@@ -392,11 +402,15 @@
 
     @pl.when(is_root)
     def _():
-        each_piece(lambda q, r: [from_root(s, u, q, r).wait_send() for s in range(2) for u in range(2)])
+        each_piece(lambda q, r: [from_root(s, u, q, r).wait_send() for s, u in ((0, 1), (0, 0), (1, 0))])
 
     @pl.when(any_seed)
     def _():
         each_piece(lambda q, r: from_seed(0, 1, q, r).wait_send())
+
+    @pl.when(seeds[0][2])
+    def _():
+        each_piece(lambda q, r: onward(q, r).wait_send())
 
     for s in range(2):
         @pl.when(any_relay[s])

time: 57.3 us -> 55.2 us (0.963)
  the two profiles are of different devices: /device:TPU:6 before, /device:TPU:1 now
where the time goes in v5:
time: 55.2 us; the launch traced here: 55 us
  Pallas kernels  52.8 us (96%)
  local copies, waits for them, and re-layouts  2.14 us (4%)
    pallas_call x1, Pallas kernels, on_device(): pl.pallas_call(kernel, out_shape=jax.ShapeDtypeStruct(loc.shape, bf), in_...  52.8 us
    unnamed x1, local copies, waits for them, and re-layouts  2.14 us

profile of v5, /device:TPU:1, one launch (start us, length us, event | category | flops | bytes accessed | tf_op | source)
XLA Modules:
  0.0 55.0 jit_solution(5754012451401400804)
XLA Ops:
  0.0 52.8 %shard_map.55 = bf16[2,2,48,2304]{3,2,1,0:T(8,128)(2,1)} custom-call(bf16[2,2,48,2304]{3,2,1,0:T(8,128)(2,1)} %bitcast.5, s32[3,8]{1,0:T(4,128)} %bitcast.6, s32[2,3]{1,0:T(2,128)} %bitcast.7, bf16[2,96,96]{2,1,0:T(8,128)(2,1)} %constant.4.clone.left_in, bf16[2,256,256]{2,1,0:T(8,128)(2,1)} %constant.5.clone.right_in), custom_call_target="tpu_custom_call" | custom-call | tf_op jit(solution)/shard_map/pallas_call | solution.py:434
  52.8 2.1 %copy.7 = bf16[1,2,2,48,2304]{4,3,2,1,0:T(8,128)(2,1)} copy(bf16[1,2,2,48,2304]{4,3,2,1,0:T(8,128)(2,1)} %bitcast.4) | data formatting | bytes 1769472

commit v6 on v5

--- a/solution.py
+++ b/solution.py
@@ -390,11 +390,11 @@
 
         phase_b(b, cc, kern.at[u // 2], left)
 
+        phase_c(cc, spr, acc, left, right)
+
         @pl.when(u == 1)
         def _():
             take(1)
-
-        phase_c(cc, spr, acc, left, right)
         return 0
 
     lax.fori_loop(0, 4, one, 0)

time: 55.2 us -> 55 us (level)
  Pallas kernels: 52.8 us -> 52.2 us
    pallas_call x1, Pallas kernels: 52.8 us -> 52.2 us  [on_device(): pl.pallas_call(kernel, out_shape=jax.ShapeDtypeStruct(loc.shape, bf), in_...]
where the time goes in v6:
time: 55 us; the launch traced here: 54.4 us
  Pallas kernels  52.2 us (95%)
  local copies, waits for them, and re-layouts  2.14 us (4%)
    pallas_call x1, Pallas kernels, on_device(): pl.pallas_call(kernel, out_shape=jax.ShapeDtypeStruct(loc.shape, bf), in_...  52.2 us
    unnamed x1, local copies, waits for them, and re-layouts  2.14 us

profile of v6, /device:TPU:1, one launch (start us, length us, event | category | flops | bytes accessed | tf_op | source)
XLA Modules:
  0.0 54.4 jit_solution(11408488614000168409)
XLA Ops:
  0.0 52.2 %shard_map.55 = bf16[2,2,48,2304]{3,2,1,0:T(8,128)(2,1)} custom-call(bf16[2,2,48,2304]{3,2,1,0:T(8,128)(2,1)} %bitcast.5, s32[3,8]{1,0:T(4,128)} %bitcast.6, s32[2,3]{1,0:T(2,128)} %bitcast.7, bf16[2,96,96]{2,1,0:T(8,128)(2,1)} %constant.4.clone.left_in, bf16[2,256,256]{2,1,0:T(8,128)(2,1)} %constant.5.clone.right_in), custom_call_target="tpu_custom_call" | custom-call | tf_op jit(solution)/shard_map/pallas_call | solution.py:434
  52.2 2.1 %copy.7 = bf16[1,2,2,48,2304]{4,3,2,1,0:T(8,128)(2,1)} copy(bf16[1,2,2,48,2304]{4,3,2,1,0:T(8,128)(2,1)} %bitcast.4) | data formatting | bytes 1769472
